TPU v7x, 32 devices: a whole 2x2x4 slice. The times are simulated.
32 devices in a mesh: inst: 8 (over z, y), tp: 4 (over x, core).
Axes of the slice: x: 2, y: 2, z: 4, core: 2. Of those that a mesh axis runs over, the one named last changes fastest.
Arguments:
- queries: bfloat16 [64, 3, 8192], P('inst', None, 'tp')
- new_kv: bfloat16 [64, 2, 3, 1024], P('inst', None, None, 'tp')
- key_value_pool: bfloat16 [960, 2, 64, 1024], P('inst', None, None, 'tp'), may hold values from -5 to 5
- ctx_len: int32 [64], P('inst'), may hold values from 257 to 960, as said below
- entry_lender: int32 [64, 5], P('inst'), may hold values from 0 to 7, as said below
- entry_blocks: int32 [64, 5], P('inst'), may hold values from 1 to 3
- entry_slot: int32 [64, 5], P('inst'), may hold values from 0 to 117, as said below
- out_weight: bfloat16 [8192, 4096], P('tp'), may hold values from -0.0625 to 0.0625
Outputs:
- attention: bfloat16 [64, 3, 8192], P('inst', None, 'tp')
- projected: bfloat16 [64, 3, 4096], P('inst', None, 'tp')
Inputs may be any that keep to these rules, and one draw needn't show every extreme that they name: `ctx_len`: A request holds ((blocks of all its entries) - 1) * 64 + 1 to (blocks of all its entries) * 64 cached tokens. `entry_lender`: entry 0 is the request's home instance, the index of inst that holds its row; the other entries name other instances. The requests of one home name one other instance in at most 6 entries, and each instance is named by exactly 8 * (4) entries of other homes' requests. entry_slot + 3 <= 120; the blocks entry_slot to entry_slot + 2 of different entries on one instance never meet.
All inputs are finite; a program needn't handle non-finite values.
Results may differ from a plain program's by a relative error of at most 0.02.
Values may be sent and summed in bfloat16 or wider, within the bound.
A program may use at most 128 MiB of HBM per device.

v0:
```python
import functools
import math

import jax
import jax.numpy as jnp
from jax import lax
from jax.experimental import pallas as pl
from jax.experimental.pallas import tpu as pltpu
from jax.sharding import PartitionSpec as P

HEAD_SIZE = 128
GROUP = 8
MOST_BLOCKS = 3
MESH = pl.DeviceIdType.MESH
SCALE = 1.0 / math.sqrt(HEAD_SIZE)


def attend(q, keys, values, seen, kv_heads):
    rows = q.shape[0]
    per = rows // kv_heads
    if kv_heads > 1:
        wide = jnp.concatenate([q] * kv_heads, axis=1)
        r = lax.broadcasted_iota(jnp.int32, wide.shape, 0) // per
        c = lax.broadcasted_iota(jnp.int32, wide.shape, 1) // HEAD_SIZE
        wide = jnp.where(r == c, wide.astype(jnp.float32), 0.0).astype(jnp.bfloat16)
    else:
        wide = q
    s = lax.dot_general(wide, keys, (((1,), (1,)), ((), ())), preferred_element_type=jnp.float32) * SCALE
    s = jnp.where(seen, s, -1e30)
    top = jnp.max(s, axis=1, keepdims=True)
    e = jnp.exp(s - top)
    total = jnp.sum(e, axis=1, keepdims=True)
    o = jnp.dot(e.astype(jnp.bfloat16), values, preferred_element_type=jnp.float32)
    if kv_heads > 1:
        o = jnp.concatenate(
            [o[a * per : (a + 1) * per, a * HEAD_SIZE : (a + 1) * HEAD_SIZE] for a in range(kv_heads)], axis=0
        )
    return o * (1.0 / total), top + jnp.log(total)


def to_rows(columns):
    pad = jnp.zeros((128 - columns.shape[0], 128), columns.dtype)
    return jnp.transpose(jnp.concatenate([columns, pad], axis=0))


def kernel(
    dims,
    ctx_ref, lender_ref, blocks_ref, slot_ref, q_ref, new_ref, pool_hbm, weight_hbm,
    att_ref, proj_ref,
    pool, weight, send_q, got_q, send_meta, got_meta, live_smem, plan_vmem, plan, send_part, got_part, send_lse,
    got_lse, home_part, spread, attn, send_y, got_y, queries, fresh_rows,
    pool_sem, weight_sem, q_send, q_recv, m_send, m_recv, smem_sem, p_send, p_recv, l_send, l_recv, y_send, y_recv,
    plan_sem,
):
    n, tps, cap, requests, steps, kv, entries = dims
    rows = kv * steps * GROUP
    block_rows = pool.shape[2]
    span = MOST_BLOCKS * block_rows
    me = lax.axis_index("inst")
    tp = lax.axis_index("tp")
    chunk = weight.shape[2]
    offsets = [n // 2 + ((i + 1) // 2) * (1 - 2 * (i % 2)) for i in range(n - 1)]

    barrier = pltpu.get_barrier_semaphore()
    for j in range(1, n):
        pl.semaphore_signal(barrier, inc=1, device_id=((me + j) % n, tp), device_id_type=MESH)
    for o in range(1, tps):
        pl.semaphore_signal(barrier, inc=1, device_id=(me, (tp + o) % tps), device_id_type=MESH)

    pool_parts = pool_sem.shape[0]
    part = pool.shape[0] // pool_parts
    pool_copies = [
        pltpu.make_async_copy(pool_hbm.at[pl.ds(i * part, part)], pool.at[pl.ds(i * part, part)], pool_sem.at[i])
        for i in range(pool_parts)
    ]
    for copy in pool_copies:
        copy.start()
    order = [tps // 2] + [o for o in range(1, tps) if o != tps // 2] + [0]
    weight_copies = {}
    for o in order:
        col = pl.multiple_of(((tp + o) % tps) * chunk, chunk)
        weight_copies[o] = pltpu.make_async_copy(weight_hbm.at[:, pl.ds(col, chunk)], weight.at[o], weight_sem.at[o])
        weight_copies[o].start()

    plan_row = lax.broadcasted_iota(jnp.int32, (n, 128), 0)
    plan_lane = lax.broadcasted_iota(jnp.int32, (n, 128), 1)
    table = jnp.zeros((n, 128), jnp.int32)
    used = jnp.zeros((n, 128), jnp.int32)
    ranks = jnp.zeros((n, 128), jnp.int32)
    home_codes, entry_offsets = [], []
    for r in range(requests):
        before = 0
        for e in range(entries):
            blocks = blocks_ref[r, e]
            live = jnp.clip(ctx_ref[r] - block_rows * before, 0, block_rows * blocks)
            before = before + blocks
            group = lax.div(slot_ref[r, e], MOST_BLOCKS)
            if e == 0:
                home_codes.append((group, live))
                continue
            away = lender_ref[r, e] - me
            away = jnp.where(away < 0, away + n, away)
            entry_offsets.append(away)
            code = r * 65536 + group * 256 + live
            hit = plan_row == away
            table = jnp.where(hit & (plan_lane == used), code, table)
            ranks = jnp.where(hit & (plan_lane == len(entry_offsets) - 1), jnp.minimum(used, cap - 1), ranks)
            used = used + jnp.where(hit, 1, 0)
    plan_vmem[0:n] = table
    plan_vmem[n : n + 8] = jnp.broadcast_to(jnp.sum(ranks, axis=0, keepdims=True), (8, 128))
    plan_copy = pltpu.make_async_copy(plan_vmem, plan, plan_sem)
    plan_copy.start()
    for j in range(1, n):
        send_meta[j] = jnp.broadcast_to(table[j : j + 1], (8, 128))

    for s in range(steps):
        for h in range(kv * GROUP):
            a, g = h // GROUP, h % GROUP
            block = q_ref[s, :, h * HEAD_SIZE : (h + 1) * HEAD_SIZE].astype(jnp.float32)
            spread[pl.ds((a * steps + s) * GROUP + g, requests, stride=rows), :] = block
    for r in range(requests):
        queries[r] = spread[r * rows : (r + 1) * rows, :].astype(jnp.bfloat16)

    plan_copy.wait()
    for j in offsets:
        for k in range(cap):
            send_q[j, k] = queries[lax.shift_right_logical(plan[j, k], 16)]
    pl.semaphore_wait(barrier, n - 1 + tps - 1)

    def q_copy(j):
        return pltpu.make_async_remote_copy(
            src_ref=send_q.at[j], dst_ref=got_q.at[j], send_sem=q_send.at[j], recv_sem=q_recv.at[j],
            device_id=((me + j) % n, tp), device_id_type=MESH,
        )

    def m_copy(j):
        return pltpu.make_async_remote_copy(
            src_ref=send_meta.at[j], dst_ref=got_meta.at[j], send_sem=m_send.at[j], recv_sem=m_recv.at[j],
            device_id=((me + j) % n, tp), device_id_type=MESH,
        )

    def p_copy(j):
        return pltpu.make_async_remote_copy(
            src_ref=send_part.at[j], dst_ref=got_part.at[j], send_sem=p_send.at[j], recv_sem=p_recv.at[j],
            device_id=((me + n - j) % n, tp), device_id_type=MESH,
        )

    def l_copy(j):
        return pltpu.make_async_remote_copy(
            src_ref=send_lse.at[j], dst_ref=got_lse.at[j], send_sem=l_send.at[j], recv_sem=l_recv.at[j],
            device_id=((me + n - j) % n, tp), device_id_type=MESH,
        )

    for j in offsets:
        m_copy(j).start()
        q_copy(j).start()
    fresh_rows[...] = jnp.zeros_like(fresh_rows)
    for r in range(requests):
        for i in range(steps):
            pair = new_ref[r, i].astype(jnp.float32)
            for c in range(2):
                fresh_rows[r, c, i : i + 1, :] = pair[c : c + 1]
    for copy in pool_copies:
        copy.wait()

    def fetch(group):
        taken = pool[pl.ds(group * MOST_BLOCKS, MOST_BLOCKS)]
        return taken[:, 0].reshape(span, kv * HEAD_SIZE), taken[:, 1].reshape(span, kv * HEAD_SIZE)

    lane = lax.broadcasted_iota(jnp.int32, (rows, 128), 1)
    fresh = fresh_rows.shape[2]
    home_col = lax.broadcasted_iota(jnp.int32, (rows, span + fresh), 1)
    home_step = (lax.broadcasted_iota(jnp.int32, (rows, span + fresh), 0) // GROUP) % steps
    own_seen = (home_col >= span) & (home_col - span <= home_step)

    home_columns = jnp.zeros((rows, 128), jnp.float32)
    for r in range(requests):
        group, live = home_codes[r]
        keys, values = fetch(group)
        keys = jnp.concatenate([keys, fresh_rows[r, 0].astype(jnp.bfloat16)], axis=0)
        values = jnp.concatenate([values, fresh_rows[r, 1].astype(jnp.bfloat16)], axis=0)
        o, lse = attend(queries[r], keys, values, (home_col < live) | own_seen, kv)
        home_part[r] = o.astype(jnp.bfloat16)
        home_columns = jnp.where(lane == r, lse, home_columns)
    home_lse = to_rows(home_columns)[:requests]

    lent_col = lax.broadcasted_iota(jnp.int32, (rows, span), 1)

    def lend(i, carry):
        j = n // 2 + ((i + 1) // 2) * (1 - 2 * (i % 2))
        m_copy(j).wait_recv()
        down = pltpu.make_async_copy(got_meta.at[j], live_smem.at[j], smem_sem.at[j])
        down.start()
        q_copy(j).wait_recv()
        down.wait()
        columns = jnp.zeros((rows, 128), jnp.float32)
        for k in range(cap):
            code = live_smem[j, 0, k]
            keys, values = fetch(lax.shift_right_logical(code, 8) & 255)
            q = got_q[j, k]
            o, lse = attend(q, keys, values, lent_col < (code & 255), kv)
            send_part[j, k] = o.astype(jnp.bfloat16)
            columns = jnp.where(lane == k, lse, columns)
        send_lse[j] = to_rows(columns)[:8]
        p_copy(j).start()
        l_copy(j).start()
        return carry

    lax.fori_loop(0, n - 1, lend, 0)

    for j in range(1, n):
        l_copy(j).wait_recv()
    logsums = [home_lse]
    for e in range(1, entries):
        picked = []
        for r in range(requests):
            item = r * (entries - 1) + e - 1
            picked.append(got_lse[entry_offsets[item], pl.ds(plan[n, item], 1), :])
        logsums.append(jnp.concatenate(picked, axis=0))
    highest = functools.reduce(jnp.maximum, logsums)
    weights = [jnp.exp(x - highest) for x in logsums]
    inverse = 1.0 / functools.reduce(jnp.add, weights)
    stacked = jnp.concatenate([w * inverse for w in weights], axis=0)
    stacked = jnp.concatenate([stacked, jnp.zeros((128 - stacked.shape[0], 128), jnp.float32)], axis=0)
    by_head = jnp.transpose(stacked)[:rows]

    for j in range(1, n):
        p_copy(j).wait_recv()
    for r in range(requests):
        total = by_head[:, r : r + 1] * home_part[r].astype(jnp.float32)
        for e in range(1, entries):
            item = r * (entries - 1) + e - 1
            far = got_part[entry_offsets[item], plan[n, item]]
            c = e * requests + r
            total = total + by_head[:, c : c + 1] * far.astype(jnp.float32)
        spread[r * rows : (r + 1) * rows, :] = total
    tokens = requests * steps
    for h in range(kv * GROUP):
        a, g = h // GROUP, h % GROUP
        block = jnp.concatenate(
            [spread[pl.ds((a * steps + s) * GROUP + g, requests, stride=rows), :] for s in range(steps)], axis=0
        )
        attn[:, h * HEAD_SIZE : (h + 1) * HEAD_SIZE] = block.astype(jnp.bfloat16)
        for s in range(steps):
            att_ref[s, :, h * HEAD_SIZE : (h + 1) * HEAD_SIZE] = block[s * requests : (s + 1) * requests].astype(
                jnp.bfloat16
            )

    def y_copy(o):
        return pltpu.make_async_remote_copy(
            src_ref=send_y.at[o], dst_ref=got_y.at[o], send_sem=y_send.at[o], recv_sem=y_recv.at[o],
            device_id=(me, (tp + o) % tps), device_id_type=MESH,
        )

    half = chunk // 2
    own = None
    for o in order:
        weight_copies[o].wait()
        y = jnp.dot(attn[...], weight[o], preferred_element_type=jnp.float32)
        y = jnp.concatenate([y[:, :half], y[:, half:]], axis=0)
        if o == 0:
            own = y
        else:
            send_y[o] = y.astype(jnp.bfloat16)
            y_copy(o).start()
    for o in order[:-1]:
        y_copy(o).wait_recv()
        own = own + got_y[o].astype(jnp.float32)
    for s in range(steps):
        proj_ref[s, :, :half] = own[s * requests : (s + 1) * requests].astype(jnp.bfloat16)
        proj_ref[s, :, half:] = own[tokens + s * requests : tokens + (s + 1) * requests].astype(jnp.bfloat16)

    for j in range(1, n):
        m_copy(j).wait_send()
        q_copy(j).wait_send()
        p_copy(j).wait_send()
        l_copy(j).wait_send()
    for o in range(1, tps):
        y_copy(o).wait_send()


def local(queries, new_kv, key_value_pool, ctx_len, entry_lender, entry_blocks, entry_slot, out_weight):
    requests, steps, query_width = queries.shape
    heads = query_width // HEAD_SIZE
    kv = key_value_pool.shape[3] // HEAD_SIZE
    entries = entry_lender.shape[1]
    n = lax.axis_size("inst")
    tps = lax.axis_size("tp")
    items = requests * (entries - 1)
    cap = 2 * ((items // 2 + n - 2) // (n - 1))
    rows = heads * steps

    tokens = requests * steps
    chunk = out_weight.shape[1] // tps
    vmem = pl.BlockSpec(memory_space=pltpu.VMEM)
    hbm = pl.BlockSpec(memory_space=pl.ANY)
    bf, f32 = jnp.bfloat16, jnp.float32
    dma = pltpu.SemaphoreType.DMA
    att, proj = pl.pallas_call(
        functools.partial(kernel, (n, tps, cap, requests, steps, kv, entries)),
        out_shape=(
            jax.ShapeDtypeStruct((steps, requests, query_width), bf),
            jax.ShapeDtypeStruct((steps, requests, chunk), bf),
        ),
        in_specs=[pl.BlockSpec(memory_space=pltpu.SMEM)] * 4 + [vmem, vmem, hbm, hbm],
        out_specs=(vmem, vmem),
        scratch_shapes=[
            pltpu.VMEM(key_value_pool.shape, bf),
            pltpu.VMEM((tps, out_weight.shape[0], chunk), bf),
            pltpu.VMEM((n, cap, rows, HEAD_SIZE), bf),
            pltpu.VMEM((n, cap, rows, HEAD_SIZE), bf),
            pltpu.VMEM((n, 8, 128), jnp.int32),
            pltpu.VMEM((n, 8, 128), jnp.int32),
            pltpu.SMEM((n, 8, 128), jnp.int32),
            pltpu.VMEM((n + 8, 128), jnp.int32),
            pltpu.SMEM((n + 8, 128), jnp.int32),
            pltpu.VMEM((n, cap, rows, HEAD_SIZE), bf),
            pltpu.VMEM((n, cap, rows, HEAD_SIZE), bf),
            pltpu.VMEM((n, 8, 128), f32),
            pltpu.VMEM((n, 8, 128), f32),
            pltpu.VMEM((requests, rows, HEAD_SIZE), bf),
            pltpu.VMEM((requests * rows, HEAD_SIZE), f32),
            pltpu.VMEM((tokens, query_width), bf),
            pltpu.VMEM((tps, 2 * tokens, chunk // 2), bf),
            pltpu.VMEM((tps, 2 * tokens, chunk // 2), bf),
            pltpu.VMEM((requests, rows, HEAD_SIZE), bf),
            pltpu.VMEM((requests, 2, 16, key_value_pool.shape[3]), f32),
            dma((4,)), dma((tps,)),
            dma((n,)), dma((n,)), dma((n,)), dma((n,)), dma((n,)),
            dma((n,)), dma((n,)), dma((n,)), dma((n,)),
            dma((tps,)), dma((tps,)), dma,
        ],
        compiler_params=pltpu.CompilerParams(
            collective_id=0, has_side_effects=True, vmem_limit_bytes=52 * 1024 * 1024
        ),
    )(
        ctx_len, entry_lender, entry_blocks, entry_slot,
        queries.transpose(1, 0, 2), new_kv.transpose(0, 2, 1, 3), key_value_pool, out_weight,
    )
    return att.transpose(1, 0, 2), proj.transpose(1, 0, 2)


def solution(mesh):
    return jax.shard_map(
        local,
        mesh=mesh,
        in_specs=(
            P("inst", None, "tp"),
            P("inst", None, None, "tp"),
            P("inst", None, None, "tp"),
            P("inst"),
            P("inst", None),
            P("inst", None),
            P("inst", None),
            P("tp", None),
        ),
        out_specs=(P("inst", None, "tp"), P("inst", None, "tp")),
        check_vma=False,
    )
```

profile of v0, /device:TPU:1, one launch (start us, length us, event | category | flops | bytes accessed | tf_op | source)
XLA Modules:
  0.0 51.7 jit_solution(10257797695133944636)
XLA Ops:
  0.6 0.0 copy-start
  0.6 0.9 %copy-done = bf16[8,3,2048]{2,0,1:T(8,128)(2,1)S(1)} copy-done((bf16[8,3,2048]{2,0,1:T(8,128)(2,1)S(1)}, bf16[8,3,2048]{2,0,1:T(8,128)(2,1)}, u32[]{:S(2)}) %copy-start) | copy-done | bytes 98328
  1.5 0.0 copy-start.1
  1.5 0.7 %copy-done.1 = bf16[8,2,3,256]{3,1,2,0:T(2,128)(2,1)S(1)} copy-done((bf16[8,2,3,256]{3,1,2,0:T(2,128)(2,1)S(1)}, bf16[8,2,3,256]{3,1,2,0:T(2,128)(2,1)}, u32[]{:S(2)}) %copy-start.1) | copy-done | bytes 24600
  2.3 0.0 copy-start.2
  2.3 0.7 %copy-done.2 = s32[8,5]{1,0:T(8,128)S(1)} copy-done((s32[8,5]{1,0:T(8,128)S(1)}, s32[8,5]{1,0:T(8,128)}, u32[]{:S(2)}) %copy-start.2) | copy-done | bytes 184
  3.0 0.0 copy-start.3
  3.0 0.7 %copy-done.3 = s32[8,5]{1,0:T(8,128)S(1)} copy-done((s32[8,5]{1,0:T(8,128)S(1)}, s32[8,5]{1,0:T(8,128)}, u32[]{:S(2)}) %copy-start.3) | copy-done | bytes 184
  3.6 0.0 copy-start.4
  3.6 0.7 %copy-done.4 = s32[8,5]{1,0:T(8,128)S(1)} copy-done((s32[8,5]{1,0:T(8,128)S(1)}, s32[8,5]{1,0:T(8,128)}, u32[]{:S(2)}) %copy-start.4) | copy-done | bytes 184
  4.3 0.0 copy-start.5
  4.3 0.7 %copy-done.5 = s32[8]{0:T(128)S(1)} copy-done((s32[8]{0:T(128)S(1)}, s32[8]{0:T(128)}, u32[]{:S(2)}) %copy-start.5) | copy-done | bytes 56
  5.0 45.5 %shard_map.95 = (bf16[3,8,2048]{2,1,0:T(8,128)(2,1)S(1)}, bf16[3,8,1024]{2,1,0:T(8,128)(2,1)S(1)}) custom-call(s32[8]{0:T(128)S(1)} %copy-done.5, s32[8,5]{1,0:T(8,128)S(1)} %copy-done.2, s32[8,5]{1,0:T(8,128)S(1)} %copy-done.3, s32[8,5]{1,0:T(8,128)S(1)} %copy-done.4, bf16[3,8,2048]{2,1,0:T(8,128)(2,1)S(1)} %bitcast.4, bf16[8,3,2,256]{3,2,1,0:T(2,128)(2,1)S(1)} %bitcast.7, ...), custom_call_target="tpu_custom_call" | custom-call | tf_op jit(solution)/shard_map/pallas_call | solution.py:299
  50.4 0.6 %copy.12 = bf16[8,3,2048]{2,0,1:T(8,128)(2,1)} copy(bf16[8,3,2048]{2,0,1:T(8,128)(2,1)S(1)} %bitcast.5) | data formatting | bytes 196608
  51.1 0.6 %copy.13 = bf16[8,3,1024]{2,0,1:T(8,128)(2,1)} copy(bf16[8,3,1024]{2,0,1:T(8,128)(2,1)S(1)} %bitcast.6) | data formatting | bytes 98304
Async XLA Ops:
  0.6 0.9 %copy-start = (bf16[8,3,2048]{2,0,1:T(8,128)(2,1)S(1)}, bf16[8,3,2048]{2,0,1:T(8,128)(2,1)}, u32[]{:S(2)}) copy-start(bf16[8,3,2048]{2,0,1:T(8,128)(2,1)} %param.8) | copy-start | bytes 294916
  1.5 0.7 %copy-start.1 = (bf16[8,2,3,256]{3,1,2,0:T(2,128)(2,1)S(1)}, bf16[8,2,3,256]{3,1,2,0:T(2,128)(2,1)}, u32[]{:S(2)}) copy-start(bf16[8,2,3,256]{3,1,2,0:T(2,128)(2,1)} %param.9) | copy-start | bytes 73732
  2.3 0.7 %copy-start.2 = (s32[8,5]{1,0:T(8,128)S(1)}, s32[8,5]{1,0:T(8,128)}, u32[]{:S(2)}) copy-start(s32[8,5]{1,0:T(8,128)} %lender_ref.1) | copy-start | bytes 484
  3.0 0.7 %copy-start.3 = (s32[8,5]{1,0:T(8,128)S(1)}, s32[8,5]{1,0:T(8,128)}, u32[]{:S(2)}) copy-start(s32[8,5]{1,0:T(8,128)} %blocks_ref.1) | copy-start | bytes 484
  3.6 0.7 %copy-start.4 = (s32[8,5]{1,0:T(8,128)S(1)}, s32[8,5]{1,0:T(8,128)}, u32[]{:S(2)}) copy-start(s32[8,5]{1,0:T(8,128)} %slot_ref.1) | copy-start | bytes 484
  4.3 0.7 %copy-start.5 = (s32[8]{0:T(128)S(1)}, s32[8]{0:T(128)}, u32[]{:S(2)}) copy-start(s32[8]{0:T(128)} %ctx_ref.1) | copy-start | bytes 100
where the time goes:
time: 52 us; the launch traced here: 51.7 us
  Pallas kernels  45.5 us (88%)
  local copies, waits for them, and re-layouts  5.6 us (11%)
  between operations  0.65 us (1%)
    pallas_call x1, Pallas kernels, local(): pl.pallas_call(functools.partial(kernel, (n, tps, cap, requests, steps, k...  45.5 us
    unnamed x14, local copies, waits for them, and re-layouts  5.6 us

commit v1 on v0

--- a/solution.py
+++ b/solution.py
@@ -45,12 +45,12 @@
 
 def kernel(
     dims,
-    ctx_ref, lender_ref, blocks_ref, slot_ref, q_ref, new_ref, pool_hbm, weight_hbm,
+    ctx_hbm, lender_hbm, blocks_hbm, slot_hbm, q_hbm, new_hbm, pool_hbm, weight_hbm,
     att_ref, proj_ref,
-    pool, weight, send_q, got_q, send_meta, got_meta, live_smem, plan_vmem, plan, send_part, got_part, send_lse,
-    got_lse, home_part, spread, attn, send_y, got_y, queries, fresh_rows,
+    pool, weight, ctx_ref, lender_ref, blocks_ref, slot_ref, q_ref, new_ref, got_q, send_meta, got_meta, live_smem, plan_vmem, plan, send_part, got_part, send_lse,
+    got_lse, home_part, spread, attn, send_y, got_y, queries, queries_in, fresh_rows,
     pool_sem, weight_sem, q_send, q_recv, m_send, m_recv, smem_sem, p_send, p_recv, l_send, l_recv, y_send, y_recv,
-    plan_sem,
+    plan_sem, in_sem,
 ):
     n, tps, cap, requests, steps, kv, entries = dims
     rows = kv * steps * GROUP
@@ -59,7 +59,18 @@
     me = lax.axis_index("inst")
     tp = lax.axis_index("tp")
     chunk = weight.shape[2]
-    offsets = [n // 2 + ((i + 1) // 2) * (1 - 2 * (i % 2)) for i in range(n - 1)]
+    outers = n // 2
+    inner = me % 2
+    partner = me + 1 - 2 * inner
+    small = [
+        pltpu.make_async_copy(src, dst, in_sem.at[i])
+        for i, (src, dst) in enumerate(
+            [(q_hbm, q_ref), (ctx_hbm, ctx_ref), (lender_hbm, lender_ref), (blocks_hbm, blocks_ref),
+             (slot_hbm, slot_ref), (new_hbm, new_ref)]
+        )
+    ]
+    for copy in small:
+        copy.start()
 
     barrier = pltpu.get_barrier_semaphore()
     for j in range(1, n):
@@ -81,6 +92,36 @@
         col = pl.multiple_of(((tp + o) % tps) * chunk, chunk)
         weight_copies[o] = pltpu.make_async_copy(weight_hbm.at[:, pl.ds(col, chunk)], weight.at[o], weight_sem.at[o])
         weight_copies[o].start()
+
+    small[0].wait()
+    for s in range(steps):
+        for h in range(kv * GROUP):
+            a, g = h // GROUP, h % GROUP
+            block = q_ref[s, :, h * HEAD_SIZE : (h + 1) * HEAD_SIZE].astype(jnp.float32)
+            spread[pl.ds((a * steps + s) * GROUP + g, requests, stride=rows), :] = block
+    for r in range(requests):
+        queries[r] = spread[r * rows : (r + 1) * rows, :].astype(jnp.bfloat16)
+
+    pl.semaphore_wait(barrier, n - 1 + tps - 1)
+
+    def q_direct(z):
+        return pltpu.make_async_remote_copy(
+            src_ref=queries, dst_ref=got_q.at[z], send_sem=q_send.at[z], recv_sem=q_recv.at[z],
+            device_id=((me + 2 * z) % n, tp), device_id_type=MESH,
+        )
+
+    def q_relay(z, src):
+        return pltpu.make_async_remote_copy(
+            src_ref=src, dst_ref=got_q.at[outers + z], send_sem=q_send.at[outers + z],
+            recv_sem=q_recv.at[outers + z], device_id=(partner, tp), device_id_type=MESH,
+        )
+
+    outer_order = [outers // 2] + [z for z in range(1, outers) if z != outers // 2]
+    for z in outer_order:
+        q_direct(z).start()
+    q_relay(0, queries).start()
+    for copy in small[1:]:
+        copy.wait()
 
     plan_row = lax.broadcasted_iota(jnp.int32, (n, 128), 0)
     plan_lane = lax.broadcasted_iota(jnp.int32, (n, 128), 1)
@@ -113,26 +154,6 @@
     for j in range(1, n):
         send_meta[j] = jnp.broadcast_to(table[j : j + 1], (8, 128))
 
-    for s in range(steps):
-        for h in range(kv * GROUP):
-            a, g = h // GROUP, h % GROUP
-            block = q_ref[s, :, h * HEAD_SIZE : (h + 1) * HEAD_SIZE].astype(jnp.float32)
-            spread[pl.ds((a * steps + s) * GROUP + g, requests, stride=rows), :] = block
-    for r in range(requests):
-        queries[r] = spread[r * rows : (r + 1) * rows, :].astype(jnp.bfloat16)
-
-    plan_copy.wait()
-    for j in offsets:
-        for k in range(cap):
-            send_q[j, k] = queries[lax.shift_right_logical(plan[j, k], 16)]
-    pl.semaphore_wait(barrier, n - 1 + tps - 1)
-
-    def q_copy(j):
-        return pltpu.make_async_remote_copy(
-            src_ref=send_q.at[j], dst_ref=got_q.at[j], send_sem=q_send.at[j], recv_sem=q_recv.at[j],
-            device_id=((me + j) % n, tp), device_id_type=MESH,
-        )
-
     def m_copy(j):
         return pltpu.make_async_remote_copy(
             src_ref=send_meta.at[j], dst_ref=got_meta.at[j], send_sem=m_send.at[j], recv_sem=m_recv.at[j],
@@ -151,9 +172,9 @@
             device_id=((me + n - j) % n, tp), device_id_type=MESH,
         )
 
-    for j in offsets:
+    for j in range(1, n):
         m_copy(j).start()
-        q_copy(j).start()
+    plan_copy.wait()
     fresh_rows[...] = jnp.zeros_like(fresh_rows)
     for r in range(requests):
         for i in range(steps):
@@ -186,27 +207,40 @@
 
     lent_col = lax.broadcasted_iota(jnp.int32, (rows, span), 1)
 
-    def lend(i, carry):
-        j = n // 2 + ((i + 1) // 2) * (1 - 2 * (i % 2))
+    def lend(slot, j):
         m_copy(j).wait_recv()
         down = pltpu.make_async_copy(got_meta.at[j], live_smem.at[j], smem_sem.at[j])
         down.start()
-        q_copy(j).wait_recv()
+        queries_in[...] = got_q[slot]
         down.wait()
         columns = jnp.zeros((rows, 128), jnp.float32)
         for k in range(cap):
             code = live_smem[j, 0, k]
             keys, values = fetch(lax.shift_right_logical(code, 8) & 255)
-            q = got_q[j, k]
+            q = queries_in[lax.shift_right_logical(code, 16)]
             o, lse = attend(q, keys, values, lent_col < (code & 255), kv)
             send_part[j, k] = o.astype(jnp.bfloat16)
             columns = jnp.where(lane == k, lse, columns)
         send_lse[j] = to_rows(columns)[:8]
         p_copy(j).start()
         l_copy(j).start()
+
+    def near(i, carry):
+        z = jnp.where(i == 1, outers // 2, jnp.where(i <= outers // 2, i - 1, i))
+        q_direct(z).wait_recv()
+        q_relay(z, got_q.at[z]).start()
+        lend(z, 2 * z)
         return carry
 
-    lax.fori_loop(0, n - 1, lend, 0)
+    def relayed(i, carry):
+        z = jnp.where(i == 1, outers // 2, jnp.where((i > 1) & (i <= outers // 2), i - 1, i))
+        q_relay(z, queries).wait_recv()
+        lend(outers + z, (2 * z - 1 + 2 * inner + n) % n)
+        return carry
+
+    relayed(0, 0)
+    lax.fori_loop(1, outers, near, 0)
+    lax.fori_loop(1, outers, relayed, 0)
 
     for j in range(1, n):
         l_copy(j).wait_recv()
@@ -272,9 +306,12 @@
 
     for j in range(1, n):
         m_copy(j).wait_send()
-        q_copy(j).wait_send()
         p_copy(j).wait_send()
         l_copy(j).wait_send()
+    for z in range(1, outers):
+        q_direct(z).wait_send()
+    for z in range(outers):
+        q_relay(z, queries).wait_send()
     for o in range(1, tps):
         y_copy(o).wait_send()
 
@@ -293,7 +330,7 @@
     tokens = requests * steps
     chunk = out_weight.shape[1] // tps
     vmem = pl.BlockSpec(memory_space=pltpu.VMEM)
-    hbm = pl.BlockSpec(memory_space=pl.ANY)
+    hbm = pl.BlockSpec(memory_space=pltpu.HBM)
     bf, f32 = jnp.bfloat16, jnp.float32
     dma = pltpu.SemaphoreType.DMA
     att, proj = pl.pallas_call(
@@ -302,13 +339,18 @@
             jax.ShapeDtypeStruct((steps, requests, query_width), bf),
             jax.ShapeDtypeStruct((steps, requests, chunk), bf),
         ),
-        in_specs=[pl.BlockSpec(memory_space=pltpu.SMEM)] * 4 + [vmem, vmem, hbm, hbm],
+        in_specs=[hbm] * 8,
         out_specs=(vmem, vmem),
         scratch_shapes=[
             pltpu.VMEM(key_value_pool.shape, bf),
             pltpu.VMEM((tps, out_weight.shape[0], chunk), bf),
-            pltpu.VMEM((n, cap, rows, HEAD_SIZE), bf),
-            pltpu.VMEM((n, cap, rows, HEAD_SIZE), bf),
+            pltpu.SMEM(ctx_len.shape, jnp.int32),
+            pltpu.SMEM(entry_lender.shape, jnp.int32),
+            pltpu.SMEM(entry_lender.shape, jnp.int32),
+            pltpu.SMEM(entry_lender.shape, jnp.int32),
+            pltpu.VMEM((steps, requests, query_width), bf),
+            pltpu.VMEM((requests, steps, 2, new_kv.shape[3]), bf),
+            pltpu.VMEM((n, requests, rows, HEAD_SIZE), bf),
             pltpu.VMEM((n, 8, 128), jnp.int32),
             pltpu.VMEM((n, 8, 128), jnp.int32),
             pltpu.SMEM((n, 8, 128), jnp.int32),
@@ -324,14 +366,15 @@
             pltpu.VMEM((tps, 2 * tokens, chunk // 2), bf),
             pltpu.VMEM((tps, 2 * tokens, chunk // 2), bf),
             pltpu.VMEM((requests, rows, HEAD_SIZE), bf),
+            pltpu.VMEM((requests, rows, HEAD_SIZE), bf),
             pltpu.VMEM((requests, 2, 16, key_value_pool.shape[3]), f32),
             dma((4,)), dma((tps,)),
             dma((n,)), dma((n,)), dma((n,)), dma((n,)), dma((n,)),
             dma((n,)), dma((n,)), dma((n,)), dma((n,)),
-            dma((tps,)), dma((tps,)), dma,
+            dma((tps,)), dma((tps,)), dma, dma((6,)),
         ],
         compiler_params=pltpu.CompilerParams(
-            collective_id=0, has_side_effects=True, vmem_limit_bytes=52 * 1024 * 1024
+            collective_id=0, has_side_effects=True, vmem_limit_bytes=64 * 1024 * 1024
         ),
     )(
         ctx_len, entry_lender, entry_blocks, entry_slot,

time: 52 us -> 45.9 us (0.88)
  Pallas kernels: 45.5 us -> 42.1 us
  local copies, waits for them, and re-layouts: 5.6 us -> 2.96 us
    pallas_call x1, Pallas kernels: 45.5 us -> 42.1 us  [local(): pl.pallas_call(functools.partial(kernel, (n, tps, cap, requests, steps, k...]
    unnamed x14 -> x2, local copies, waits for them, and re-layouts: 5.6 us -> 2.96 us
where the time goes in v1:
time: 45.9 us; the launch traced here: 45.7 us
  Pallas kernels  42.1 us (92%)
  local copies, waits for them, and re-layouts  2.96 us (6%)
  between operations  0.64 us (1%)
    pallas_call x1, Pallas kernels, local(): pl.pallas_call(functools.partial(kernel, (n, tps, cap, requests, steps, k...  42.1 us
    unnamed x2, local copies, waits for them, and re-layouts  2.96 us

profile of v1, /device:TPU:1, one launch (start us, length us, event | category | flops | bytes accessed | tf_op | source)
XLA Modules:
  0.0 45.7 jit_solution(6010335651705341526)
XLA Ops:
  0.6 42.1 %shard_map.95 = (bf16[3,8,2048]{2,1,0:T(8,128)(2,1)}, bf16[3,8,1024]{2,1,0:T(8,128)(2,1)}) custom-call(s32[8]{0:T(128)} %ctx_hbm.1, s32[8,5]{1,0:T(8,128)} %lender_hbm.1, s32[8,5]{1,0:T(8,128)} %blocks_hbm.1, s32[8,5]{1,0:T(8,128)} %slot_hbm.1, bf16[3,8,2048]{2,1,0:T(8,128)(2,1)} %bitcast.4, bf16[8,3,2,256]{3,2,1,0:T(2,128)(2,1)} %bitcast.7, ...), custom_call_target="tpu_custom_call" | custom-call | tf_op jit(solution)/shard_map/pallas_call | solution.py:336
  42.8 1.5 %copy.12 = bf16[8,3,2048]{2,0,1:T(8,128)(2,1)} copy(bf16[8,3,2048]{2,0,1:T(8,128)(2,1)} %bitcast.5) | data formatting | bytes 196608
  44.3 1.4 %copy.13 = bf16[8,3,1024]{2,0,1:T(8,128)(2,1)} copy(bf16[8,3,1024]{2,0,1:T(8,128)(2,1)} %bitcast.6) | data formatting | bytes 98304

commit v2 on v1

--- a/solution.py
+++ b/solution.py
@@ -116,8 +116,13 @@
             recv_sem=q_recv.at[outers + z], device_id=(partner, tp), device_id_type=MESH,
         )
 
-    outer_order = [outers // 2] + [z for z in range(1, outers) if z != outers // 2]
-    for z in outer_order:
+    def q_forward(z):
+        return pltpu.make_async_remote_copy(
+            src_ref=got_q.at[z - 1], dst_ref=got_q.at[z], send_sem=q_send.at[z], recv_sem=q_recv.at[z],
+            device_id=((me + 2) % n, tp), device_id_type=MESH,
+        )
+
+    for z in sorted({1, outers - 1}):
         q_direct(z).start()
     q_relay(0, queries).start()
     for copy in small[1:]:
@@ -226,14 +231,19 @@
         l_copy(j).start()
 
     def near(i, carry):
-        z = jnp.where(i == 1, outers // 2, jnp.where(i <= outers // 2, i - 1, i))
+        z = jnp.where(i == 1, 1, jnp.where(i == 2, outers - 1, i - 1))
         q_direct(z).wait_recv()
+
+        @pl.when(z + 1 < outers - 1)
+        def _():
+            q_forward(z + 1).start()
+
         q_relay(z, got_q.at[z]).start()
         lend(z, 2 * z)
         return carry
 
     def relayed(i, carry):
-        z = jnp.where(i == 1, outers // 2, jnp.where((i > 1) & (i <= outers // 2), i - 1, i))
+        z = jnp.where(i <= 1, i, jnp.where(i == 2, outers - 1, i - 1))
         q_relay(z, queries).wait_recv()
         lend(outers + z, (2 * z - 1 + 2 * inner + n) % n)
         return carry
@@ -336,8 +346,8 @@
     att, proj = pl.pallas_call(
         functools.partial(kernel, (n, tps, cap, requests, steps, kv, entries)),
         out_shape=(
-            jax.ShapeDtypeStruct((steps, requests, query_width), bf),
-            jax.ShapeDtypeStruct((steps, requests, chunk), bf),
+            pltpu.VMEM((steps, requests, query_width), bf),
+            pltpu.VMEM((steps, requests, chunk), bf),
         ),
         in_specs=[hbm] * 8,
         out_specs=(vmem, vmem),
@@ -374,7 +384,7 @@
             dma((tps,)), dma((tps,)), dma, dma((6,)),
         ],
         compiler_params=pltpu.CompilerParams(
-            collective_id=0, has_side_effects=True, vmem_limit_bytes=64 * 1024 * 1024
+            collective_id=0, has_side_effects=True, vmem_limit_bytes=60 * 1024 * 1024
         ),
     )(
         ctx_len, entry_lender, entry_blocks, entry_slot,

time: 45.9 us -> 43.6 us (0.950)
  local copies, waits for them, and re-layouts: 2.96 us -> 1.26 us
  Pallas kernels: 42.1 us -> 41.5 us
    unnamed x2, local copies, waits for them, and re-layouts: 2.96 us -> 1.26 us
    pallas_call x1, Pallas kernels: 42.1 us -> 41.5 us  [local(): pl.pallas_call(functools.partial(kernel, (n, tps, cap, requests, steps, k...]
where the time goes in v2:
time: 43.6 us; the launch traced here: 43.4 us
  Pallas kernels  41.5 us (95%)
  local copies, waits for them, and re-layouts  1.26 us (3%)
  between operations  0.64 us (1%)
    pallas_call x1, Pallas kernels, local(): pl.pallas_call(functools.partial(kernel, (n, tps, cap, requests, steps, k...  41.5 us
    unnamed x2, local copies, waits for them, and re-layouts  1.26 us

profile of v2, /device:TPU:1, one launch (start us, length us, event | category | flops | bytes accessed | tf_op | source)
XLA Modules:
  0.0 43.4 jit_solution(5731671414768576154)
XLA Ops:
  0.6 41.5 %shard_map.95 = (bf16[3,8,2048]{2,1,0:T(8,128)(2,1)S(1)}, bf16[3,8,1024]{2,1,0:T(8,128)(2,1)S(1)}) custom-call(s32[8]{0:T(128)} %ctx_hbm.1, s32[8,5]{1,0:T(8,128)} %lender_hbm.1, s32[8,5]{1,0:T(8,128)} %blocks_hbm.1, s32[8,5]{1,0:T(8,128)} %slot_hbm.1, bf16[3,8,2048]{2,1,0:T(8,128)(2,1)} %bitcast.6, bf16[8,3,2,256]{3,2,1,0:T(2,128)(2,1)} %bitcast.7, ...), custom_call_target="tpu_custom_call" | custom-call | tf_op jit(solution)/shard_map/pallas_call | solution.py:346
  42.2 0.6 %copy.12 = bf16[8,3,2048]{2,0,1:T(8,128)(2,1)} copy(bf16[8,3,2048]{2,0,1:T(8,128)(2,1)S(1)} %bitcast.4) | data formatting | bytes 196608
  42.8 0.6 %copy.13 = bf16[8,3,1024]{2,0,1:T(8,128)(2,1)} copy(bf16[8,3,1024]{2,0,1:T(8,128)(2,1)S(1)} %bitcast.5) | data formatting | bytes 98304

commit v3 on v2

--- a/solution.py
+++ b/solution.py
@@ -86,12 +86,6 @@
     ]
     for copy in pool_copies:
         copy.start()
-    order = [tps // 2] + [o for o in range(1, tps) if o != tps // 2] + [0]
-    weight_copies = {}
-    for o in order:
-        col = pl.multiple_of(((tp + o) % tps) * chunk, chunk)
-        weight_copies[o] = pltpu.make_async_copy(weight_hbm.at[:, pl.ds(col, chunk)], weight.at[o], weight_sem.at[o])
-        weight_copies[o].start()
 
     small[0].wait()
     for s in range(steps):
@@ -121,6 +115,15 @@
             src_ref=got_q.at[z - 1], dst_ref=got_q.at[z], send_sem=q_send.at[z], recv_sem=q_recv.at[z],
             device_id=((me + 2) % n, tp), device_id_type=MESH,
         )
+
+    def arrive(z):
+        q_direct(z).wait_recv()
+
+        @pl.when(z + 1 < outers - 1)
+        def _():
+            q_forward(z + 1).start()
+
+        q_relay(z, got_q.at[z]).start()
 
     for z in sorted({1, outers - 1}):
         q_direct(z).start()
@@ -188,6 +191,12 @@
                 fresh_rows[r, c, i : i + 1, :] = pair[c : c + 1]
     for copy in pool_copies:
         copy.wait()
+    order = [tps // 2] + [o for o in range(1, tps) if o != tps // 2] + [0]
+    weight_copies = {}
+    for o in order:
+        col = pl.multiple_of(((tp + o) % tps) * chunk, chunk)
+        weight_copies[o] = pltpu.make_async_copy(weight_hbm.at[:, pl.ds(col, chunk)], weight.at[o], weight_sem.at[o])
+        weight_copies[o].start()
 
     def fetch(group):
         taken = pool[pl.ds(group * MOST_BLOCKS, MOST_BLOCKS)]
@@ -200,7 +209,11 @@
     own_seen = (home_col >= span) & (home_col - span <= home_step)
 
     home_columns = jnp.zeros((rows, 128), jnp.float32)
+    early = sorted({1, outers - 1})
     for r in range(requests):
+        if r in (requests // 2, requests - 1):
+            for z in early[:1] if r == requests // 2 else early[1:]:
+                arrive(z)
         group, live = home_codes[r]
         keys, values = fetch(group)
         keys = jnp.concatenate([keys, fresh_rows[r, 0].astype(jnp.bfloat16)], axis=0)
@@ -232,13 +245,11 @@
 
     def near(i, carry):
         z = jnp.where(i == 1, 1, jnp.where(i == 2, outers - 1, i - 1))
-        q_direct(z).wait_recv()
-
-        @pl.when(z + 1 < outers - 1)
+
+        @pl.when(i > 2)
         def _():
-            q_forward(z + 1).start()
-
-        q_relay(z, got_q.at[z]).start()
+            arrive(z)
+
         lend(z, 2 * z)
         return carry
 

time: 43.6 us -> 42.2 us (0.968)
  Pallas kernels: 41.5 us -> 40.1 us
    pallas_call x1, Pallas kernels: 41.5 us -> 40.1 us  [local(): pl.pallas_call(functools.partial(kernel, (n, tps, cap, requests, steps, k...]
where the time goes in v3:
time: 42.2 us; the launch traced here: 42 us
  Pallas kernels  40.1 us (95%)
  local copies, waits for them, and re-layouts  1.26 us (3%)
  between operations  0.64 us (2%)
    pallas_call x1, Pallas kernels, local(): pl.pallas_call(functools.partial(kernel, (n, tps, cap, requests, steps, k...  40.1 us
    unnamed x2, local copies, waits for them, and re-layouts  1.26 us

profile of v3, /device:TPU:1, one launch (start us, length us, event | category | flops | bytes accessed | tf_op | source)
XLA Modules:
  0.0 42.0 jit_solution(7192832858149219551)
XLA Ops:
  0.6 40.1 %shard_map.95 = (bf16[3,8,2048]{2,1,0:T(8,128)(2,1)S(1)}, bf16[3,8,1024]{2,1,0:T(8,128)(2,1)S(1)}) custom-call(s32[8]{0:T(128)} %ctx_hbm.1, s32[8,5]{1,0:T(8,128)} %lender_hbm.1, s32[8,5]{1,0:T(8,128)} %blocks_hbm.1, s32[8,5]{1,0:T(8,128)} %slot_hbm.1, bf16[3,8,2048]{2,1,0:T(8,128)(2,1)} %bitcast.6, bf16[8,3,2,256]{3,2,1,0:T(2,128)(2,1)} %bitcast.7, ...), custom_call_target="tpu_custom_call" | custom-call | tf_op jit(solution)/shard_map/pallas_call | solution.py:357
  40.7 0.6 %copy.12 = bf16[8,3,2048]{2,0,1:T(8,128)(2,1)} copy(bf16[8,3,2048]{2,0,1:T(8,128)(2,1)S(1)} %bitcast.4) | data formatting | bytes 196608
  41.3 0.6 %copy.13 = bf16[8,3,1024]{2,0,1:T(8,128)(2,1)} copy(bf16[8,3,1024]{2,0,1:T(8,128)(2,1)S(1)} %bitcast.5) | data formatting | bytes 98304

commit v4 on v3

--- a/solution.py
+++ b/solution.py
@@ -221,16 +221,18 @@
         o, lse = attend(queries[r], keys, values, (home_col < live) | own_seen, kv)
         home_part[r] = o.astype(jnp.bfloat16)
         home_columns = jnp.where(lane == r, lse, home_columns)
+    downs = [pltpu.make_async_copy(got_meta.at[j], live_smem.at[j], smem_sem.at[j]) for j in range(1, n)]
+    for j in range(1, n):
+        m_copy(j).wait_recv()
+        downs[j - 1].start()
     home_lse = to_rows(home_columns)[:requests]
+    for down in downs:
+        down.wait()
 
     lent_col = lax.broadcasted_iota(jnp.int32, (rows, span), 1)
 
     def lend(slot, j):
-        m_copy(j).wait_recv()
-        down = pltpu.make_async_copy(got_meta.at[j], live_smem.at[j], smem_sem.at[j])
-        down.start()
         queries_in[...] = got_q[slot]
-        down.wait()
         columns = jnp.zeros((rows, 128), jnp.float32)
         for k in range(cap):
             code = live_smem[j, 0, k]
@@ -240,8 +242,8 @@
             send_part[j, k] = o.astype(jnp.bfloat16)
             columns = jnp.where(lane == k, lse, columns)
         send_lse[j] = to_rows(columns)[:8]
+        l_copy(j).start()
         p_copy(j).start()
-        l_copy(j).start()
 
     def near(i, carry):
         z = jnp.where(i == 1, 1, jnp.where(i == 2, outers - 1, i - 1))

time: 42.2 us -> 42.4 us (level)
  no operation moved by 1% of the time
where the time goes in v4:
time: 42.4 us; the launch traced here: 42.3 us
  Pallas kernels  40.4 us (95%)
  local copies, waits for them, and re-layouts  1.26 us (3%)
  between operations  0.64 us (2%)
    pallas_call x1, Pallas kernels, local(): pl.pallas_call(functools.partial(kernel, (n, tps, cap, requests, steps, k...  40.4 us
    unnamed x2, local copies, waits for them, and re-layouts  1.26 us

profile of v4, /device:TPU:1, one launch (start us, length us, event | category | flops | bytes accessed | tf_op | source)
XLA Modules:
  0.0 42.3 jit_solution(16937980113406433211)
XLA Ops:
  0.6 40.4 %shard_map.95 = (bf16[3,8,2048]{2,1,0:T(8,128)(2,1)S(1)}, bf16[3,8,1024]{2,1,0:T(8,128)(2,1)S(1)}) custom-call(s32[8]{0:T(128)} %ctx_hbm.1, s32[8,5]{1,0:T(8,128)} %lender_hbm.1, s32[8,5]{1,0:T(8,128)} %blocks_hbm.1, s32[8,5]{1,0:T(8,128)} %slot_hbm.1, bf16[3,8,2048]{2,1,0:T(8,128)(2,1)} %bitcast.6, bf16[8,3,2,256]{3,2,1,0:T(2,128)(2,1)} %bitcast.7, ...), custom_call_target="tpu_custom_call" | custom-call | tf_op jit(solution)/shard_map/pallas_call | solution.py:359
  41.0 0.6 %copy.12 = bf16[8,3,2048]{2,0,1:T(8,128)(2,1)} copy(bf16[8,3,2048]{2,0,1:T(8,128)(2,1)S(1)} %bitcast.4) | data formatting | bytes 196608
  41.6 0.6 %copy.13 = bf16[8,3,1024]{2,0,1:T(8,128)(2,1)} copy(bf16[8,3,1024]{2,0,1:T(8,128)(2,1)S(1)} %bitcast.5) | data formatting | bytes 98304
